TPU v7x, 32 devices: a whole 2x2x4 slice. The times are simulated.
32 devices in a mesh: dist: 4 (over x, core), ctr: 8 (over z, y).
Axes of the slice: x: 2, y: 2, z: 4, core: 2. Of those that a mesh axis runs over, the one named last changes fastest.
Arguments:
- three_centre: bfloat16 [1024, 4, 4096], P(('dist', 'ctr')), may hold values from -0.359375 to 0.359375
- occupied_green: bfloat16 [128, 4096], P(('dist', 'ctr')), may hold values from -0.75 to 0.75
- virtual_green: bfloat16 [128, 4096], P(('dist', 'ctr')), may hold values from -0.75 to 0.75
- pair_index: int32 [16, 4], replicated, may hold values from 0 to 7, as said below
- source_slot: int32 [16, 4, 4], replicated, may hold values from -1 to 3, as said below
- occupied_index: int32 [16, 4, 4], replicated, may hold values from 0 to 127, as said below
- virtual_index: int32 [16, 4, 4], replicated, may hold values from 0 to 127, as said below
Outputs:
- density_response: float32 [1024, 256], P(('dist', 'ctr'))
Inputs may be any that keep to these rules, and one draw needn't show every extreme that they name: `pair_index`: the 4 entries of a row are distinct. `source_slot`: for each slot the listed slots are distinct and come first, followed by -1 entries; all slots of one auxiliary atom list the same number of slots, at least 1; in every draw some auxiliary atom lists 4. `occupied_index`: for auxiliary atom p with g = p // 4, every entry lies in g * 32 to g * 32 + 2 * 32 - 1, taken modulo 128. `virtual_index`: for auxiliary atom p with g = p // 4, every entry lies in g * 32 to g * 32 + 2 * 32 - 1, taken modulo 128.
All inputs are finite; a program needn't handle non-finite values.
Results may differ from a plain program's by a relative error of at most 0.004.
Values may be sent and summed in bfloat16 or wider, within the bound.
A program may use at most 64 MiB of HBM per device.

v0:
```python
import jax
import jax.numpy as jnp
from jax import lax
from jax.sharding import PartitionSpec as P

BLK = 64
AUXB = 64
NPR = 8


def shifted(block, axis, distance):
    devices = range(lax.axis_size(axis))
    route = [((i - distance) % len(devices), i) for i in devices]
    return lax.ppermute(block, axis, route)


def shards(
    three_centre,
    occupied_green,
    virtual_green,
    pair_index,
    source_slot,
    occupied_index,
    virtual_index,
):
    row_count = three_centre.shape[0]
    slot_count = three_centre.shape[1]
    ctr_size = lax.axis_size("ctr")
    dist_size = lax.axis_size("dist")
    dist_index = lax.axis_index("dist")
    ctr_index = lax.axis_index("ctr")
    flat_index = dist_index * ctr_size + ctr_index
    atom_index = flat_index * row_count // AUXB
    source_rows = lax.dynamic_index_in_dim(source_slot, atom_index, 0, keepdims=False)
    occ_ids = lax.dynamic_index_in_dim(occupied_index, atom_index, 0, keepdims=False)
    virt_ids = lax.dynamic_index_in_dim(virtual_index, atom_index, 0, keepdims=False)
    occ_own, virt_own = (
        lax.all_gather(occupied_green, "ctr", axis=0, tiled=True),
        lax.all_gather(virtual_green, "ctr", axis=0, tiled=True),
    )
    following = shifted(jnp.stack([occ_own, virt_own]), "dist", -1)
    occ_table = jnp.concatenate([occ_own, following[0]], axis=0)
    virt_table = jnp.concatenate([virt_own, following[1]], axis=0)
    region_base = dist_index * occ_own.shape[0]
    list_total = occ_own.shape[0] * dist_size
    occ_position = jnp.mod(occ_ids - region_base, list_total)
    virt_position = jnp.mod(virt_ids - region_base, list_total)
    tensor_rows = three_centre.reshape(row_count, slot_count, BLK, BLK)
    accumulated = jnp.zeros(tensor_rows.shape, jnp.float32)
    for step in range(source_rows.shape[1]):
        source_col = source_rows[:, step]
        live_mask = (source_col >= 0).astype(jnp.float32)
        picked = jnp.take(tensor_rows, jnp.maximum(source_col, 0), axis=1)
        virt_blocks = jnp.take(virt_table, virt_position[:, step], axis=0).reshape(
            slot_count, BLK, BLK
        )
        product = jnp.einsum(
            "aslv,svz->aslz", picked, virt_blocks, preferred_element_type=jnp.float32
        )
        product = (product * live_mask[None, :, None, None]).astype(jnp.bfloat16)
        occ_blocks = jnp.take(occ_table, occ_position[:, step], axis=0).reshape(
            slot_count, BLK, BLK
        )
        accumulated = accumulated + jnp.einsum(
            "slm,aslz->asmz", occ_blocks, product, preferred_element_type=jnp.float32
        )
    updated = accumulated.astype(jnp.bfloat16).reshape(row_count, slot_count, BLK * BLK)
    upd_region, ten_region = (
        lax.all_to_all(updated, "ctr", split_axis=2, concat_axis=0, tiled=True),
        lax.all_to_all(three_centre, "ctr", split_axis=2, concat_axis=0, tiled=True),
    )
    region_rows = upd_region.shape[0]
    col_count = upd_region.shape[2]
    region_atoms = region_rows // AUXB
    region_pairs = lax.dynamic_slice_in_dim(pair_index, dist_index * region_atoms, region_atoms, 0)
    one_hot = (region_pairs[:, :, None] == jnp.arange(NPR)[None, None, :]).astype(jnp.bfloat16)
    upd_blocks = upd_region.reshape(region_atoms, AUXB, slot_count, col_count)
    ten_blocks = ten_region.reshape(region_atoms, AUXB, slot_count, col_count)
    upd_space = (
        jnp.einsum("psk,pasc->kpac", one_hot, upd_blocks, preferred_element_type=jnp.float32)
        .astype(jnp.bfloat16)
        .reshape(NPR, region_rows, col_count)
    )
    ten_space = (
        jnp.einsum("psk,pasc->kpac", one_hot, ten_blocks, preferred_element_type=jnp.float32)
        .astype(jnp.bfloat16)
        .reshape(NPR, region_rows, col_count)
    )
    return lax.psum_scatter(
        jnp.einsum("kac,kbc->ab", upd_space, ten_space, preferred_element_type=jnp.float32),
        "ctr",
        scatter_dimension=0,
        tiled=True,
    )


def solution(mesh):
    return jax.shard_map(
        shards,
        mesh=mesh,
        in_specs=(
            P(("dist", "ctr"), None, None),
            P(("dist", "ctr"), None),
            P(("dist", "ctr"), None),
            P(),
            P(),
            P(),
            P(),
        ),
        out_specs=P(("dist", "ctr"), None),
        check_vma=False,
    )
```

profile of v0, /device:TPU:0, one launch (start us, length us, event | category | flops | bytes accessed | tf_op | source)
XLA Modules:
  0.0 265.6 jit_solution(9622120785204081876)
XLA Ops:
  6.5 32.9 %all-gather.1 = bf16[8,4,4096]{2,1,0:T(4,128)(2,1)S(1)} all-gather(bf16[1,4,4096]{2,1,0:T(4,128)(2,1)} %bitcast.126), channel_id=1, replica_groups=mesh['dist'=4,'ctr'=8] {'ctr'}, dimensions={0}, use_global_device_ids=true | all-gather | bytes 294912 | tf_op jit(solution)/shard_map/all_gather | solution.py:38
  39.4 30.9 %all-gather = bf16[8,4,4096]{2,1,0:T(4,128)(2,1)S(1)} all-gather(bf16[1,4,4096]{2,1,0:T(4,128)(2,1)} %bitcast.127), channel_id=1, replica_groups=mesh['dist'=4,'ctr'=8] {'ctr'}, dimensions={0}, use_global_device_ids=true | all-gather | bytes 294912 | tf_op jit(solution)/shard_map/all_gather | solution.py:39
  70.5 0.8 pad_maximum_fusion
  71.3 4.8 %copy.40 = bf16[32,4,4096]{0,1,2:T(4,128)(2,1)} copy(bf16[32,4,4096]{2,1,0:T(4,128)(2,1)S(1)} %copy-done.3) | data formatting | bytes 2097152 | tf_op args[0]
  76.2 7.8 %reshape.296 = bf16[8,2,32768]{2,1,0:T(2,128)(2,1)} reshape(bf16[4096,4,32]{2,1,0:T(4,128)(2,1)} %bitcast.120) | data formatting | bytes 2097152
  84.0 5.7 %all-to-all-start.1 = ((bf16[8,2,32768]{2,1,0:T(2,128)(2,1)}), bf16[8,2,32768]{2,1,0:T(2,128)(2,1)}, u32[]{:S(2)}, u32[]{:S(2)}) async-start(bf16[8,2,32768]{2,1,0:T(2,128)(2,1)} %reshape.296), calls=%async_computation.1 | async-start | bytes 2097152 | tf_op jit(solution)/shard_map/all_to_all | solution.py:70
  91.4 0.8 reshape.236
  92.2 1.8 reshape.108
  94.3 2.2 gather_fusion.10
  96.4 2.2 gather_fusion.7
  98.6 2.2 gather_fusion.4
  100.8 2.1 gather_fusion.1
  103.0 1.1 slice_bitcast_fusion
  104.0 1.0 pad_maximum_fusion.1
  105.1 0.6 gather_fusion.9
  111.5 4.7 %fusion.2 = f32[4,32,64,64]{3,2,1,0:T(8,128)} fusion(bf16[4,32,64,64]{3,2,1,0:T(8,128)(2,1)S(1)} %copy-done.2, f32[4]{0:T(128)S(1)} %get-tuple-element.18, pred[4]{0:T(512)(128)(4,1)S(1)} %get-tuple-element.41, bf16[4,64,64]{2,1,0:T(8,128)(2,1)S(1)} %reshape.112, bf16[4,64,64,1]{2,1,0,3:T(8,128)(2,1)S(1)} %reshape.268), kind=kOutput, calls=%fused_computation.19 | convolution fusion | flops 135790592 | bytes 3211284 | tf_op jit(solution)/shard_map/slm,aslz->asmz/dot_general | solution.py:64
  116.2 6.5 %fusion.8 = f32[4,32,64,64]{3,2,1,0:T(8,128)} fusion(bf16[4,32,64,64]{3,2,1,0:T(8,128)(2,1)} %gather_fusion.1, f32[4]{0:T(128)S(1)} %get-tuple-element.16, pred[4]{0:T(512)(128)(4,1)S(1)} %get-tuple-element.47, bf16[4,64,64]{2,1,0:T(8,128)(2,1)S(1)} %reshape.107, bf16[4,64,64,1]{2,1,0,3:T(8,128)(2,1)S(1)} %reshape.264), kind=kOutput, calls=%fused_computation.25 | convolution fusion | flops 135790592 | bytes 3211284 | tf_op jit(solution)/shard_map/slm,aslz->asmz/dot_general | solution.py:64
  122.6 4.7 %fusion.5 = f32[4,32,64,64]{3,2,1,0:T(8,128)} fusion(bf16[4,32,64,64]{3,2,1,0:T(8,128)(2,1)S(1)} %copy-done.1, f32[4]{0:T(128)S(1)} %get-tuple-element.17, pred[4]{0:T(512)(128)(4,1)S(1)} %get-tuple-element.44, bf16[4,64,64]{2,1,0:T(8,128)(2,1)S(1)} %reshape.110, bf16[4,64,64,1]{2,1,0,3:T(8,128)(2,1)S(1)} %reshape.266), kind=kOutput, calls=%fused_computation.22 | convolution fusion | flops 135790592 | bytes 3211284 | tf_op jit(solution)/shard_map/slm,aslz->asmz/dot_general | solution.py:64
  127.4 8.2 %fusion.22 = bf16[32,4,64,64]{2,3,0,1:T(8,128)(2,1)S(1)} fusion(f32[4,32,64,64]{3,2,1,0:T(8,128)} %fusion.2, f32[4,32,64,64]{3,2,1,0:T(8,128)} %fusion.8, f32[4,32,64,64]{3,2,1,0:T(8,128)} %fusion.5, bf16[4,32,64,64]{3,2,1,0:T(8,128)(2,1)} %gather_fusion.10, f32[4]{0:T(128)S(1)} %get-tuple-element.15, pred[4]{0:T(512)(128)(4,1)S(1)} %get-tuple-element.38, ...), kind=kOutput, calls=%fused_computation.41 | convolution fusion | flops 137887744 | bytes 8454164 | tf_op jit(solution)/shard_map/slm,aslz->asmz/dot_general | solution.py:64
  135.6 7.8 %copy.61 = bf16[32,4,64,64]{0,1,3,2:T(4,128)(2,1)} copy(bf16[32,4,64,64]{2,3,0,1:T(8,128)(2,1)S(1)} %fusion.22) | data formatting | bytes 2097152 | tf_op jit(solution)/shard_map/reshape | solution.py:67
  143.4 7.8 %reshape.298 = bf16[8,2,32768]{2,1,0:T(2,128)(2,1)} reshape(bf16[4096,4,32]{2,1,0:T(4,128)(2,1)} %bitcast.117) | data formatting | bytes 2097152
  151.2 6.1 %all-to-all-start = ((bf16[8,2,32768]{2,1,0:T(2,128)(2,1)}), bf16[8,2,32768]{2,1,0:T(2,128)(2,1)S(1)}, u32[]{:S(2)}, u32[]{:S(2)}) async-start(bf16[8,2,32768]{2,1,0:T(2,128)(2,1)} %reshape.298), calls=%async_computation | async-start | bytes 2097152 | tf_op jit(solution)/shard_map/all_to_all | solution.py:69
  157.6 7.0 %reshape.297 = bf16[4096,4,32]{2,1,0:T(4,128)(2,1)} reshape(bf16[8,2,32768]{2,1,0:T(2,128)(2,1)} %all-to-all-done.1) | data formatting | bytes 2097152
  164.6 6.1 %copy.41 = bf16[32,4,8,512]{3,1,0,2:T(4,128)(2,1)S(1)} copy(bf16[32,4,8,512]{0,1,3,2:T(4,128)(2,1)} %bitcast.118) | data formatting | bytes 2097152 | tf_op jit(solution)/shard_map/all_to_all | solution.py:70
  170.8 2.2 convolution_convert_fusion
  173.0 10.2 %all-to-all-done = bf16[8,2,32768]{2,1,0:T(2,128)(2,1)S(1)} async-done(((bf16[8,2,32768]{2,1,0:T(2,128)(2,1)}), bf16[8,2,32768]{2,1,0:T(2,128)(2,1)S(1)}, u32[]{:S(2)}, u32[]{:S(2)}) %all-to-all-start) | async-done | bytes 1048608 | tf_op jit(solution)/shard_map/all_to_all | solution.py:69
  183.2 4.5 %reshape.299 = bf16[4096,4,32]{2,1,0:T(4,128)(2,1)} reshape(bf16[8,2,32768]{2,1,0:T(2,128)(2,1)S(1)} %all-to-all-done) | data formatting | bytes 2097152
  187.8 4.7 %copy.62 = bf16[32,4,8,512]{3,2,0,1:T(8,128)(2,1)S(1)} copy(bf16[32,4,8,512]{0,1,3,2:T(4,128)(2,1)} %bitcast.119) | data formatting | bytes 2097152 | tf_op jit(solution)/shard_map/all_to_all | solution.py:69
  192.4 0.8 copy.38
  193.3 1.0 convolution_convert_fusion.1
  194.9 3.0 %fusion.41 = f32[256,256]{1,0:T(8,128)} fusion(bf16[8,256,512]{2,0,1:T(8,128)(2,1)S(1)} %bitcast.124, bf16[8,256,512]{2,0,1:T(8,128)(2,1)S(1)} %bitcast.125), kind=kOutput, calls=%fused_computation.42 | convolution fusion | flops 536870912 | bytes 4456448 | tf_op jit(solution)/shard_map/kac,kbc->ab/dot_general | solution.py:90
  197.9 60.9 %reduce-scatter.2.cloned.1.call-done = f32[32,256]{1,0:T(8,128)} async-done(((f32[256,256]{1,0:T(8,128)}), f32[32,256]{1,0:T(8,128)}) %reduce-scatter.2.cloned.1.call-update) | async-done | bytes 32784 | tf_op jit(solution)/shard_map/reduce_scatter | solution.py:89
  (82 shorter events, 8.4 us)
Async XLA Ops:
  6.5 83.2 %copy-start = (s32[16,4,4]{0,2,1:T(4,128)S(1)}, s32[16,4,4]{0,2,1:T(4,128)}, u32[]{:S(2)}) copy-start(s32[16,4,4]{0,2,1:T(4,128)} %param.15) | copy-start | bytes 3076
  6.5 64.8 %copy-start.3 = (bf16[32,4,4096]{2,1,0:T(4,128)(2,1)S(1)}, bf16[32,4,4096]{2,1,0:T(4,128)(2,1)}, u32[]{:S(2)}) copy-start(bf16[32,4,4096]{2,1,0:T(4,128)(2,1)} %param.11) | copy-start | bytes 3145732
  71.3 31.6 %collective-permute-start = (bf16[2,32,4096]{2,1,0:T(8,128)(2,1)}, bf16[2,32,4096]{2,1,0:T(8,128)(2,1)}, u32[]{:S(2)}, u32[]{:S(2)}) collective-permute-start(bf16[2,32,4096]{2,1,0:T(8,128)(2,1)} %pad_maximum_fusion), channel_id=1, source_target_pairs={{8,0},{16,8},{24,16},{0,24},{9,1},{17,9},{25,17},{1,25},{10,2},{18... | collective-permute-start | bytes 1572872 | tf_op jit(solution)/shard_map/ppermute | solution.py:14
  84.0 6.3 %copy-start.5 = (s32[16,4,4]{0,2,1:T(4,128)S(1)}, s32[16,4,4]{0,2,1:T(4,128)}, u32[]{:S(2)}) copy-start(s32[16,4,4]{0,2,1:T(4,128)} %param.16) | copy-start | bytes 3076
  84.0 6.8 %copy-start.6 = (s32[16,4,4]{0,2,1:T(4,128)S(1)}, s32[16,4,4]{0,2,1:T(4,128)}, u32[]{:S(2)}) copy-start(s32[16,4,4]{0,2,1:T(4,128)} %param.17) | copy-start | bytes 3076
  84.0 67.2 %all-to-all-start.1 = ((bf16[8,2,32768]{2,1,0:T(2,128)(2,1)}), bf16[8,2,32768]{2,1,0:T(2,128)(2,1)}, u32[]{:S(2)}, u32[]{:S(2)}) async-start(bf16[8,2,32768]{2,1,0:T(2,128)(2,1)} %reshape.296), calls=%async_computation.1 | async-start | bytes 2097152 | tf_op jit(solution)/shard_map/all_to_all | solution.py:70
  105.1 6.4 %copy-start.2 = (bf16[4,32,64,64]{3,2,1,0:T(8,128)(2,1)S(1)}, bf16[4,32,64,64]{3,2,1,0:T(8,128)(2,1)}, u32[]{:S(2)}) copy-start(bf16[4,32,64,64]{3,2,1,0:T(8,128)(2,1)} %gather_fusion.7) | copy-start | bytes 3145732
  116.2 6.5 %copy-start.1 = (bf16[4,32,64,64]{3,2,1,0:T(8,128)(2,1)S(1)}, bf16[4,32,64,64]{3,2,1,0:T(8,128)(2,1)}, u32[]{:S(2)}) copy-start(bf16[4,32,64,64]{3,2,1,0:T(8,128)(2,1)} %gather_fusion.4) | copy-start | bytes 3145732
  151.2 6.2 %copy-start.7 = (s32[16,4]{0,1:T(4,128)S(1)}, s32[16,4]{0,1:T(4,128)}, u32[]{:S(2)}) copy-start(s32[16,4]{0,1:T(4,128)} %param.14) | copy-start | bytes 772
  151.2 32.0 %all-to-all-start = ((bf16[8,2,32768]{2,1,0:T(2,128)(2,1)}), bf16[8,2,32768]{2,1,0:T(2,128)(2,1)S(1)}, u32[]{:S(2)}, u32[]{:S(2)}) async-start(bf16[8,2,32768]{2,1,0:T(2,128)(2,1)} %reshape.298), calls=%async_computation | async-start | bytes 2097152 | tf_op jit(solution)/shard_map/all_to_all | solution.py:69
  157.4 101.4 %reduce-scatter.2.cloned.1.call-start = ((), (), s32[]{:S(2)}) async-start(), calls=%async_computation.3 | async-start | bytes 294912 | tf_op jit(solution)/shard_map/reduce_scatter | solution.py:89
  193.3 1.6 copy-start.4
Sparse Core Ops, SparseCore 0:
  198.0 60.7 reduce-scatter.1
where the time goes:
time: 267 us; the launch traced here: 266 us
  waiting for transfers between devices  71.2 us (27%)
  local copies, waits for them, and re-layouts  71.1 us (27%)
  blocking collectives  63.8 us (24%)
  matrix products  30.3 us (11%)
  between operations  13.8 us (5%)
  starting transfers between devices  11.9 us (4%)
  other arithmetic  3.61 us (1%)
    reduce_scatter x1, waiting for transfers between devices, shards(): lax.psum_scatter(jnp.einsum('kac,kbc->ab', upd_space, ten_space, preferre...  60.9 us
    unnamed x23, local copies, waits for them, and re-layouts  33.5 us
    all_gather x1, blocking collectives, shards(): lax.all_gather(occupied_green, 'ctr', axis=0, tiled=True)  32.9 us
    all_gather x1, blocking collectives, shards(): lax.all_gather(virtual_green, 'ctr', axis=0, tiled=True)  30.9 us
    dot_general x4, matrix products, shards(): jnp.einsum('slm,aslz->asmz', occ_blocks, product, preferred_element_type=...  24.1 us
    all_to_all x1, waiting for transfers between devices, shards(): lax.all_to_all(updated, 'ctr', split_axis=2, concat_axis=0, tiled=True)  10.2 us
    gather x4, local copies, waits for them, and re-layouts, shards(): picked = jnp.take(tensor_rows, jnp.maximum(source_col, 0), axis=1)  8.66 us
    reshape x1, local copies, waits for them, and re-layouts, shards(): accumulated.astype(jnp.bfloat16).reshape(row_count, slot_count, BLK * BLK)  7.84 us
  transfers between devices with their start and end apart: 4, of which 2 were waited for; matrix products, arithmetic and copies ran while one was open for 34% of the time, Pallas kernels for 0%

commit v1 on v0

--- a/solution.py
+++ b/solution.py
@@ -6,6 +6,16 @@
 BLK = 64
 AUXB = 64
 NPR = 8
+
+
+def collect(x, axis, dim):
+    ways, here, lap = (lax.axis_size(axis), lax.axis_index(axis), x.shape[dim])
+    shape = [n * ways if d == dim else n for d, n in enumerate(x.shape)]
+    full = lax.dynamic_update_slice_in_dim(jnp.zeros(shape, x.dtype), x, here * lap, axis=dim)
+    for far in range(1, ways):
+        x = lax.ppermute(x, axis, [(d, (d + 1) % ways) for d in range(ways)])
+        full = lax.dynamic_update_slice_in_dim(full, x, (here - far) % ways * lap, axis=dim)
+    return full
 
 
 def shifted(block, axis, distance):
@@ -36,7 +46,7 @@
     virt_ids = lax.dynamic_index_in_dim(virtual_index, atom_index, 0, keepdims=False)
     occ_own, virt_own = (
         lax.all_gather(occupied_green, "ctr", axis=0, tiled=True),
-        lax.all_gather(virtual_green, "ctr", axis=0, tiled=True),
+        collect(virtual_green, "ctr", 0),
     )
     following = shifted(jnp.stack([occ_own, virt_own]), "dist", -1)
     occ_table = jnp.concatenate([occ_own, following[0]], axis=0)

time: 267 us -> 295 us (1.10)
  waiting for transfers between devices: 71.2 us -> 118 us
  blocking collectives: 63.8 us -> 39.2 us
  other arithmetic: 3.61 us -> 6.91 us
    ppermute x0 -> x7, waiting for transfers between devices: none -> 39.6 us  [collect(): x = lax.ppermute(x, axis, [(d, (d + 1) % ways) for d in range(ways)])]
    all_gather x1 -> x0, blocking collectives: 30.9 us -> none  [shards(): lax.all_gather(virtual_green, 'ctr', axis=0, tiled=True)]
    ppermute x1, waiting for transfers between devices: 0.01 us -> 6.63 us  [shifted(): return lax.ppermute(block, axis, route)]
    all_gather x1, blocking collectives: 32.9 us -> 39.2 us  [shards(): lax.all_gather(occupied_green, 'ctr', axis=0, tiled=True)]
    ppermute x0 -> x7, starting transfers between devices: none -> 2.98 us  [collect(): x = lax.ppermute(x, axis, [(d, (d + 1) % ways) for d in range(ways)])]
    unnamed x23 -> x48, local copies, waits for them, and re-layouts: 33.5 us -> 35.9 us
  transfers between devices with their start and end apart: 4 -> 11, of which waited for: 2 -> 9; matrix products, arithmetic and copies ran while one was open for 34% -> 32% of each run, Pallas kernels for 0% -> 0%
where the time goes in v1:
time: 295 us; the launch traced here: 294 us
  waiting for transfers between devices  118 us (40%)
  local copies, waits for them, and re-layouts  72.9 us (25%)
  blocking collectives  39.2 us (13%)
  matrix products  30.3 us (10%)
  between operations  14.1 us (5%)
  starting transfers between devices  12.2 us (4%)
  other arithmetic  6.91 us (2%)
    reduce_scatter x1, waiting for transfers between devices, shards(): lax.psum_scatter(jnp.einsum('kac,kbc->ab', upd_space, ten_space, preferre...  61.1 us
    ppermute x7, waiting for transfers between devices, collect(): x = lax.ppermute(x, axis, [(d, (d + 1) % ways) for d in range(ways)])  39.6 us
    all_gather x1, blocking collectives, shards(): lax.all_gather(occupied_green, 'ctr', axis=0, tiled=True)  39.2 us
    unnamed x48, local copies, waits for them, and re-layouts  35.9 us
    dot_general x4, matrix products, shards(): jnp.einsum('slm,aslz->asmz', occ_blocks, product, preferred_element_type=...  24.1 us
    all_to_all x1, waiting for transfers between devices, shards(): lax.all_to_all(updated, 'ctr', split_axis=2, concat_axis=0, tiled=True)  10.8 us
    gather x4, local copies, waits for them, and re-layouts, shards(): picked = jnp.take(tensor_rows, jnp.maximum(source_col, 0), axis=1)  8.66 us
    reshape x1, local copies, waits for them, and re-layouts, shards(): accumulated.astype(jnp.bfloat16).reshape(row_count, slot_count, BLK * BLK)  7.62 us
  transfers between devices with their start and end apart: 11, of which 9 were waited for; matrix products, arithmetic and copies ran while one was open for 32% of the time, Pallas kernels for 0%

profile of v1, /device:TPU:0, one launch (start us, length us, event | category | flops | bytes accessed | tf_op | source)
XLA Modules:
  0.0 293.8 jit_solution(12433683958976642255)
XLA Ops:
  6.5 3.0 %collective-permute-start = (bf16[4,4096]{1,0:T(4,128)(2,1)}, bf16[4,4096]{1,0:T(4,128)(2,1)S(1)}, u32[]{:S(2)}, u32[]{:S(2)}) collective-permute-start(bf16[4,4096]{1,0:T(4,128)(2,1)} %param.13), channel_id=1, source_target_pairs={{0,1},{1,2},{2,3},{3,4},{4,5},{5,6},{6,7},{7,0},{8,9},{9,10},{10,1... | collective-permute-start | bytes 98312 | tf_op jit(solution)/shard_map/ppermute | solution.py:16
  9.5 7.2 %copy.40 = bf16[32,4,4096]{0,1,2:T(4,128)(2,1)} copy(bf16[32,4,4096]{2,1,0:T(4,128)(2,1)} %param.11) | data formatting | bytes 2097152 | tf_op args[0]
  16.7 7.8 %reshape.293 = bf16[8,2,32768]{2,1,0:T(2,128)(2,1)} reshape(bf16[4096,4,32]{2,1,0:T(4,128)(2,1)} %bitcast.120) | data formatting | bytes 2097152
  24.6 5.0 %all-to-all-start.1 = ((bf16[8,2,32768]{2,1,0:T(2,128)(2,1)}), bf16[8,2,32768]{2,1,0:T(2,128)(2,1)}, u32[]{:S(2)}, u32[]{:S(2)}) async-start(bf16[8,2,32768]{2,1,0:T(2,128)(2,1)} %reshape.293), calls=%async_computation.1 | async-start | bytes 2097152 | tf_op jit(solution)/shard_map/all_to_all | solution.py:80
  36.5 39.2 %all-gather = bf16[8,4,4096]{2,1,0:T(4,128)(2,1)S(1)} all-gather(bf16[1,4,4096]{2,1,0:T(4,128)(2,1)S(1)} %bitcast.127), channel_id=1, replica_groups=mesh['dist'=4,'ctr'=8] {'ctr'}, dimensions={0}, use_global_device_ids=true | all-gather | bytes 294912 | tf_op jit(solution)/shard_map/all_gather | solution.py:48
  77.4 1.6 reshape.108
  79.1 2.2 gather_fusion.10
  81.3 2.2 gather_fusion.7
  83.4 2.2 gather_fusion.4
  85.6 2.1 gather_fusion.1
  87.8 6.7 %collective-permute-done.1 = bf16[4,4096]{1,0:T(4,128)(2,1)S(1)} collective-permute-done((bf16[4,4096]{1,0:T(4,128)(2,1)S(1)}, bf16[4,4096]{1,0:T(4,128)(2,1)S(1)}, u32[]{:S(2)}, u32[]{:S(2)}) %collective-permute-start.1) | collective-permute-done | bytes 32800 | tf_op jit(solution)/shard_map/ppermute | solution.py:16
  94.5 6.6 %collective-permute-done.2 = bf16[4,4096]{1,0:T(4,128)(2,1)S(1)} collective-permute-done((bf16[4,4096]{1,0:T(4,128)(2,1)S(1)}, bf16[4,4096]{1,0:T(4,128)(2,1)S(1)}, u32[]{:S(2)}, u32[]{:S(2)}) %collective-permute-start.2) | collective-permute-done | bytes 32800 | tf_op jit(solution)/shard_map/ppermute | solution.py:16
  101.2 6.6 %collective-permute-done.3 = bf16[4,4096]{1,0:T(4,128)(2,1)S(1)} collective-permute-done((bf16[4,4096]{1,0:T(4,128)(2,1)S(1)}, bf16[4,4096]{1,0:T(4,128)(2,1)S(1)}, u32[]{:S(2)}, u32[]{:S(2)}) %collective-permute-start.3) | collective-permute-done | bytes 32800 | tf_op jit(solution)/shard_map/ppermute | solution.py:16
  107.8 6.6 %collective-permute-done.4 = bf16[4,4096]{1,0:T(4,128)(2,1)S(1)} collective-permute-done((bf16[4,4096]{1,0:T(4,128)(2,1)S(1)}, bf16[4,4096]{1,0:T(4,128)(2,1)S(1)}, u32[]{:S(2)}, u32[]{:S(2)}) %collective-permute-start.4) | collective-permute-done | bytes 32800 | tf_op jit(solution)/shard_map/ppermute | solution.py:16
  114.4 6.6 %collective-permute-done.5 = bf16[4,4096]{1,0:T(4,128)(2,1)S(1)} collective-permute-done((bf16[4,4096]{1,0:T(4,128)(2,1)S(1)}, bf16[4,4096]{1,0:T(4,128)(2,1)S(1)}, u32[]{:S(2)}, u32[]{:S(2)}) %collective-permute-start.5) | collective-permute-done | bytes 32800 | tf_op jit(solution)/shard_map/ppermute | solution.py:16
  121.0 6.6 %collective-permute-done.6 = bf16[4,4096]{1,0:T(4,128)(2,1)S(1)} collective-permute-done((bf16[4,4096]{1,0:T(4,128)(2,1)S(1)}, bf16[4,4096]{1,0:T(4,128)(2,1)S(1)}, u32[]{:S(2)}, u32[]{:S(2)}) %collective-permute-start.6) | collective-permute-done | bytes 32800 | tf_op jit(solution)/shard_map/ppermute | solution.py:16
  128.0 6.6 %collective-permute-done.7 = bf16[2,32,4096]{2,1,0:T(8,128)(2,1)S(1)} collective-permute-done((bf16[2,32,4096]{2,1,0:T(8,128)(2,1)S(1)}, bf16[2,32,4096]{2,1,0:T(8,128)(2,1)S(1)}, u32[]{:S(2)}, u32[]{:S(2)}) %collective-permute-start.7) | collective-permute-done | bytes 524320 | tf_op jit(solution)/shard_map/ppermute | solution.py:24
  141.3 4.7 %fusion.2 = f32[4,32,64,64]{3,2,1,0:T(8,128)} fusion(bf16[4,32,64,64]{3,2,1,0:T(8,128)(2,1)S(1)} %copy-done.2, f32[4]{0:T(128)S(1)} %get-tuple-element.18, pred[4]{0:T(512)(128)(4,1)S(1)} %get-tuple-element.32, bf16[4,64,64]{2,1,0:T(8,128)(2,1)S(1)} %reshape.112, bf16[4,64,64,1]{2,1,0,3:T(8,128)(2,1)S(1)} %reshape.265), kind=kOutput, calls=%fused_computation.19 | convolution fusion | flops 135790592 | bytes 3211284 | tf_op jit(solution)/shard_map/slm,aslz->asmz/dot_general | solution.py:74
  146.0 6.4 %fusion.8 = f32[4,32,64,64]{3,2,1,0:T(8,128)} fusion(bf16[4,32,64,64]{3,2,1,0:T(8,128)(2,1)} %gather_fusion.1, f32[4]{0:T(128)S(1)} %get-tuple-element.16, pred[4]{0:T(512)(128)(4,1)S(1)} %get-tuple-element.34, bf16[4,64,64]{2,1,0:T(8,128)(2,1)S(1)} %reshape.107, bf16[4,64,64,1]{2,1,0,3:T(8,128)(2,1)S(1)} %reshape.261), kind=kOutput, calls=%fused_computation.25 | convolution fusion | flops 135790592 | bytes 3211284 | tf_op jit(solution)/shard_map/slm,aslz->asmz/dot_general | solution.py:74
  152.4 4.7 %fusion.5 = f32[4,32,64,64]{3,2,1,0:T(8,128)} fusion(bf16[4,32,64,64]{3,2,1,0:T(8,128)(2,1)S(1)} %copy-done.1, f32[4]{0:T(128)S(1)} %get-tuple-element.17, pred[4]{0:T(512)(128)(4,1)S(1)} %get-tuple-element.33, bf16[4,64,64]{2,1,0:T(8,128)(2,1)S(1)} %reshape.110, bf16[4,64,64,1]{2,1,0,3:T(8,128)(2,1)S(1)} %reshape.263), kind=kOutput, calls=%fused_computation.22 | convolution fusion | flops 135790592 | bytes 3211284 | tf_op jit(solution)/shard_map/slm,aslz->asmz/dot_general | solution.py:74
  157.2 8.2 %fusion.22 = bf16[32,4,64,64]{2,3,0,1:T(8,128)(2,1)S(1)} fusion(f32[4,32,64,64]{3,2,1,0:T(8,128)} %fusion.2, f32[4,32,64,64]{3,2,1,0:T(8,128)} %fusion.8, f32[4,32,64,64]{3,2,1,0:T(8,128)} %fusion.5, bf16[4,32,64,64]{3,2,1,0:T(8,128)(2,1)} %gather_fusion.10, f32[4]{0:T(128)S(1)} %get-tuple-element.15, pred[4]{0:T(512)(128)(4,1)S(1)} %get-tuple-element.31, ...), kind=kOutput, calls=%fused_computation.41 | convolution fusion | flops 137887744 | bytes 8454164 | tf_op jit(solution)/shard_map/slm,aslz->asmz/dot_general | solution.py:74
  165.4 7.6 %copy.61 = bf16[32,4,64,64]{0,1,3,2:T(4,128)(2,1)} copy(bf16[32,4,64,64]{2,3,0,1:T(8,128)(2,1)S(1)} %fusion.22) | data formatting | bytes 2097152 | tf_op jit(solution)/shard_map/reshape | solution.py:77
  173.0 7.8 %reshape.295 = bf16[8,2,32768]{2,1,0:T(2,128)(2,1)} reshape(bf16[4096,4,32]{2,1,0:T(4,128)(2,1)} %bitcast.117) | data formatting | bytes 2097152
  180.8 3.7 %all-to-all-start = ((bf16[8,2,32768]{2,1,0:T(2,128)(2,1)}), bf16[8,2,32768]{2,1,0:T(2,128)(2,1)S(1)}, u32[]{:S(2)}, u32[]{:S(2)}) async-start(bf16[8,2,32768]{2,1,0:T(2,128)(2,1)} %reshape.295), calls=%async_computation | async-start | bytes 2097152 | tf_op jit(solution)/shard_map/all_to_all | solution.py:79
  185.0 7.0 %reshape.294 = bf16[4096,4,32]{2,1,0:T(4,128)(2,1)} reshape(bf16[8,2,32768]{2,1,0:T(2,128)(2,1)} %all-to-all-done.1) | data formatting | bytes 2097152
  192.0 6.1 %copy.41 = bf16[32,4,8,512]{3,1,0,2:T(4,128)(2,1)S(1)} copy(bf16[32,4,8,512]{0,1,3,2:T(4,128)(2,1)} %bitcast.118) | data formatting | bytes 2097152 | tf_op jit(solution)/shard_map/all_to_all | solution.py:80
  198.1 2.2 convolution_convert_fusion
  200.4 10.8 %all-to-all-done = bf16[8,2,32768]{2,1,0:T(2,128)(2,1)S(1)} async-done(((bf16[8,2,32768]{2,1,0:T(2,128)(2,1)}), bf16[8,2,32768]{2,1,0:T(2,128)(2,1)S(1)}, u32[]{:S(2)}, u32[]{:S(2)}) %all-to-all-start) | async-done | bytes 1048608 | tf_op jit(solution)/shard_map/all_to_all | solution.py:79
  211.2 4.5 %reshape.296 = bf16[4096,4,32]{2,1,0:T(4,128)(2,1)} reshape(bf16[8,2,32768]{2,1,0:T(2,128)(2,1)S(1)} %all-to-all-done) | data formatting | bytes 2097152
  215.8 4.7 %copy.62 = bf16[32,4,8,512]{3,2,0,1:T(8,128)(2,1)S(1)} copy(bf16[32,4,8,512]{0,1,3,2:T(4,128)(2,1)} %bitcast.119) | data formatting | bytes 2097152 | tf_op jit(solution)/shard_map/all_to_all | solution.py:79
  222.9 3.0 %fusion.41 = f32[256,256]{1,0:T(8,128)} fusion(bf16[8,256,512]{2,0,1:T(8,128)(2,1)S(1)} %bitcast.125, bf16[8,256,512]{2,0,1:T(8,128)(2,1)S(1)} %bitcast.126), kind=kOutput, calls=%fused_computation.42 | convolution fusion | flops 536870912 | bytes 4456448 | tf_op jit(solution)/shard_map/kac,kbc->ab/dot_general | solution.py:100
  225.8 61.1 %reduce-scatter.2.cloned.1.call-done = f32[32,256]{1,0:T(8,128)} async-done(((f32[256,256]{1,0:T(8,128)}), f32[32,256]{1,0:T(8,128)}) %reduce-scatter.2.cloned.1.call-update) | async-done | bytes 32784 | tf_op jit(solution)/shard_map/reduce_scatter | solution.py:99
  (135 shorter events, 18.2 us)
Async XLA Ops:
  6.5 29.1 %copy-start = (s32[16,4,4]{0,2,1:T(4,128)S(1)}, s32[16,4,4]{0,2,1:T(4,128)}, u32[]{:S(2)}) copy-start(s32[16,4,4]{0,2,1:T(4,128)} %param.15) | copy-start | bytes 3076
  6.5 81.2 %collective-permute-start = (bf16[4,4096]{1,0:T(4,128)(2,1)}, bf16[4,4096]{1,0:T(4,128)(2,1)S(1)}, u32[]{:S(2)}, u32[]{:S(2)}) collective-permute-start(bf16[4,4096]{1,0:T(4,128)(2,1)} %param.13), channel_id=1, source_target_pairs={{0,1},{1,2},{2,3},{3,4},{4,5},{5,6},{6,7},{7,0},{8,9},{9,10},{10,1... | collective-permute-start | bytes 98312 | tf_op jit(solution)/shard_map/ppermute | solution.py:16
  24.6 5.0 %copy-start.9 = (s32[16,4,4]{0,2,1:T(4,128)S(1)}, s32[16,4,4]{0,2,1:T(4,128)}, u32[]{:S(2)}) copy-start(s32[16,4,4]{0,2,1:T(4,128)} %param.16) | copy-start | bytes 3076
  24.6 5.3 %copy-start.10 = (s32[16,4,4]{0,2,1:T(4,128)S(1)}, s32[16,4,4]{0,2,1:T(4,128)}, u32[]{:S(2)}) copy-start(s32[16,4,4]{0,2,1:T(4,128)} %param.17) | copy-start | bytes 3076
  24.6 11.9 %copy-start.7 = (bf16[4,4096]{1,0:T(4,128)(2,1)S(1)}, bf16[4,4096]{1,0:T(4,128)(2,1)}, u32[]{:S(2)}) copy-start(bf16[4,4096]{1,0:T(4,128)(2,1)} %param.12) | copy-start | bytes 98308
  24.6 51.1 %copy-start.8 = (bf16[4,4096]{1,0:T(4,128)(2,1)S(1)}, bf16[4,4096]{1,0:T(4,128)(2,1)}, u32[]{:S(2)}) copy-start(bf16[4,4096]{1,0:T(4,128)(2,1)} %param.13) | copy-start | bytes 98308
  24.6 52.9 %copy-start.3 = (bf16[32,4,4096]{2,1,0:T(4,128)(2,1)S(1)}, bf16[32,4,4096]{2,1,0:T(4,128)(2,1)}, u32[]{:S(2)}) copy-start(bf16[32,4,4096]{2,1,0:T(4,128)(2,1)} %param.11) | copy-start | bytes 3145732
  24.6 156.2 %all-to-all-start.1 = ((bf16[8,2,32768]{2,1,0:T(2,128)(2,1)}), bf16[8,2,32768]{2,1,0:T(2,128)(2,1)}, u32[]{:S(2)}, u32[]{:S(2)}) async-start(bf16[8,2,32768]{2,1,0:T(2,128)(2,1)} %reshape.293), calls=%async_computation.1 | async-start | bytes 2097152 | tf_op jit(solution)/shard_map/all_to_all | solution.py:80
  85.6 42.0 %copy-start.5 = (bf16[1,32,4096]{2,1,0:T(8,128)(2,1)S(1)}, bf16[1,32,4096]{2,1,0:T(8,128)(2,1)}, u32[]{:S(2)}) copy-start(bf16[1,32,4096]{2,1,0:T(8,128)(2,1)} %stack.9) | copy-start | bytes 786436
  85.6 42.3 %copy-start.20 = (s32[4]{0:T(128)S(1)}, s32[4]{0:T(128)}, u32[]{:S(2)}) copy-start(s32[4]{0:T(128)} %compare_select_fusion) | copy-start | bytes 52
  87.7 46.9 %copy-start.6 = (bf16[32,4096]{1,0:T(8,128)(2,1)S(1)}, bf16[32,4096]{1,0:T(8,128)(2,1)}, u32[]{:S(2)}) copy-start(bf16[32,4096]{1,0:T(8,128)(2,1)} %reshape.234) | copy-start | bytes 786436
  87.7 6.8 %collective-permute-start.1 = (bf16[4,4096]{1,0:T(4,128)(2,1)S(1)}, bf16[4,4096]{1,0:T(4,128)(2,1)S(1)}, u32[]{:S(2)}, u32[]{:S(2)}) collective-permute-start(bf16[4,4096]{1,0:T(4,128)(2,1)S(1)} %collective-permute-done), channel_id=1, source_target_pairs={{0,1},{1,2},{2,3},{3,4},{4,5},{5,6},{6,7},{7,0},{8,9},{9,10},{10,1... | collective-permute-start | bytes 98312 | tf_op jit(solution)/shard_map/ppermute | solution.py:16
  94.5 6.6 %collective-permute-start.2 = (bf16[4,4096]{1,0:T(4,128)(2,1)S(1)}, bf16[4,4096]{1,0:T(4,128)(2,1)S(1)}, u32[]{:S(2)}, u32[]{:S(2)}) collective-permute-start(bf16[4,4096]{1,0:T(4,128)(2,1)S(1)} %collective-permute-done.1), channel_id=1, source_target_pairs={{0,1},{1,2},{2,3},{3,4},{4,5},{5,6},{6,7},{7,0},{8,9},{9,10},{10,1... | collective-permute-start | bytes 98312 | tf_op jit(solution)/shard_map/ppermute | solution.py:16
  101.1 6.6 %collective-permute-start.3 = (bf16[4,4096]{1,0:T(4,128)(2,1)S(1)}, bf16[4,4096]{1,0:T(4,128)(2,1)S(1)}, u32[]{:S(2)}, u32[]{:S(2)}) collective-permute-start(bf16[4,4096]{1,0:T(4,128)(2,1)S(1)} %collective-permute-done.2), channel_id=1, source_target_pairs={{0,1},{1,2},{2,3},{3,4},{4,5},{5,6},{6,7},{7,0},{8,9},{9,10},{10,1... | collective-permute-start | bytes 98312 | tf_op jit(solution)/shard_map/ppermute | solution.py:16
  107.7 6.6 %collective-permute-start.4 = (bf16[4,4096]{1,0:T(4,128)(2,1)S(1)}, bf16[4,4096]{1,0:T(4,128)(2,1)S(1)}, u32[]{:S(2)}, u32[]{:S(2)}) collective-permute-start(bf16[4,4096]{1,0:T(4,128)(2,1)S(1)} %collective-permute-done.3), channel_id=1, source_target_pairs={{0,1},{1,2},{2,3},{3,4},{4,5},{5,6},{6,7},{7,0},{8,9},{9,10},{10,1... | collective-permute-start | bytes 98312 | tf_op jit(solution)/shard_map/ppermute | solution.py:16
  114.3 6.6 %collective-permute-start.5 = (bf16[4,4096]{1,0:T(4,128)(2,1)S(1)}, bf16[4,4096]{1,0:T(4,128)(2,1)S(1)}, u32[]{:S(2)}, u32[]{:S(2)}) collective-permute-start(bf16[4,4096]{1,0:T(4,128)(2,1)S(1)} %collective-permute-done.4), channel_id=1, source_target_pairs={{0,1},{1,2},{2,3},{3,4},{4,5},{5,6},{6,7},{7,0},{8,9},{9,10},{10,1... | collective-permute-start | bytes 98312 | tf_op jit(solution)/shard_map/ppermute | solution.py:16
  121.0 6.6 %collective-permute-start.6 = (bf16[4,4096]{1,0:T(4,128)(2,1)S(1)}, bf16[4,4096]{1,0:T(4,128)(2,1)S(1)}, u32[]{:S(2)}, u32[]{:S(2)}) collective-permute-start(bf16[4,4096]{1,0:T(4,128)(2,1)S(1)} %collective-permute-done.5), channel_id=1, source_target_pairs={{0,1},{1,2},{2,3},{3,4},{4,5},{5,6},{6,7},{7,0},{8,9},{9,10},{10,1... | collective-permute-start | bytes 98312 | tf_op jit(solution)/shard_map/ppermute | solution.py:16
  127.7 6.9 %collective-permute-start.7 = (bf16[2,32,4096]{2,1,0:T(8,128)(2,1)S(1)}, bf16[2,32,4096]{2,1,0:T(8,128)(2,1)S(1)}, u32[]{:S(2)}, u32[]{:S(2)}) collective-permute-start(bf16[2,32,4096]{2,1,0:T(8,128)(2,1)S(1)} %pad_maximum_fusion), channel_id=1, source_target_pairs={{8,0},{16,8},{24,16},{0,24},{9,1},{17,9},{25,17},{1,25},{10,2},{18... | collective-permute-start | bytes 1572872 | tf_op jit(solution)/shard_map/ppermute | solution.py:24
  134.7 4.9 %copy-start.18 = (pred[4]{0:T(512)(128)(4,1)S(1)}, pred[4]{0:T(512)(128)(4,1)}, u32[]{:S(2)}) copy-start(pred[4]{0:T(512)(128)(4,1)} %compare_and_fusion.6) | copy-start | bytes 16
  134.7 5.1 %copy-start.16 = (pred[4]{0:T(512)(128)(4,1)S(1)}, pred[4]{0:T(512)(128)(4,1)}, u32[]{:S(2)}) copy-start(pred[4]{0:T(512)(128)(4,1)} %compare_and_fusion.9) | copy-start | bytes 16
  134.7 5.3 %copy-start.14 = (pred[4]{0:T(512)(128)(4,1)S(1)}, pred[4]{0:T(512)(128)(4,1)}, u32[]{:S(2)}) copy-start(pred[4]{0:T(512)(128)(4,1)} %compare_and_fusion.3) | copy-start | bytes 16
  134.7 5.5 %copy-start.12 = (pred[4]{0:T(512)(128)(4,1)S(1)}, pred[4]{0:T(512)(128)(4,1)}, u32[]{:S(2)}) copy-start(pred[4]{0:T(512)(128)(4,1)} %compare_and_fusion) | copy-start | bytes 16
  134.7 5.7 %copy-start.19 = (pred[4]{0:T(512)(128)(4,1)S(1)}, pred[4]{0:T(512)(128)(4,1)}, u32[]{:S(2)}) copy-start(pred[4]{0:T(512)(128)(4,1)} %compare_and_fusion.8) | copy-start | bytes 16
  134.8 5.8 %copy-start.17 = (pred[4]{0:T(512)(128)(4,1)S(1)}, pred[4]{0:T(512)(128)(4,1)}, u32[]{:S(2)}) copy-start(pred[4]{0:T(512)(128)(4,1)} %compare_and_fusion.11) | copy-start | bytes 16
  134.8 6.0 %copy-start.15 = (pred[4]{0:T(512)(128)(4,1)S(1)}, pred[4]{0:T(512)(128)(4,1)}, u32[]{:S(2)}) copy-start(pred[4]{0:T(512)(128)(4,1)} %compare_and_fusion.5) | copy-start | bytes 16
  134.8 6.2 %copy-start.13 = (pred[4]{0:T(512)(128)(4,1)S(1)}, pred[4]{0:T(512)(128)(4,1)}, u32[]{:S(2)}) copy-start(pred[4]{0:T(512)(128)(4,1)} %compare_and_fusion.2) | copy-start | bytes 16
  134.8 6.5 %copy-start.2 = (bf16[4,32,64,64]{3,2,1,0:T(8,128)(2,1)S(1)}, bf16[4,32,64,64]{3,2,1,0:T(8,128)(2,1)}, u32[]{:S(2)}) copy-start(bf16[4,32,64,64]{3,2,1,0:T(8,128)(2,1)} %gather_fusion.7) | copy-start | bytes 3145732
  146.0 6.5 %copy-start.1 = (bf16[4,32,64,64]{3,2,1,0:T(8,128)(2,1)S(1)}, bf16[4,32,64,64]{3,2,1,0:T(8,128)(2,1)}, u32[]{:S(2)}) copy-start(bf16[4,32,64,64]{3,2,1,0:T(8,128)(2,1)} %gather_fusion.4) | copy-start | bytes 3145732
  180.8 4.0 %copy-start.11 = (s32[16,4]{0,1:T(4,128)S(1)}, s32[16,4]{0,1:T(4,128)}, u32[]{:S(2)}) copy-start(s32[16,4]{0,1:T(4,128)} %param.14) | copy-start | bytes 772
  180.8 30.4 %all-to-all-start = ((bf16[8,2,32768]{2,1,0:T(2,128)(2,1)}), bf16[8,2,32768]{2,1,0:T(2,128)(2,1)S(1)}, u32[]{:S(2)}, u32[]{:S(2)}) async-start(bf16[8,2,32768]{2,1,0:T(2,128)(2,1)} %reshape.295), calls=%async_computation | async-start | bytes 2097152 | tf_op jit(solution)/shard_map/all_to_all | solution.py:79
  184.5 102.5 %reduce-scatter.2.cloned.1.call-start = ((), (), s32[]{:S(2)}) async-start(), calls=%async_computation.3 | async-start | bytes 294912 | tf_op jit(solution)/shard_map/reduce_scatter | solution.py:99
  221.3 1.6 copy-start.4
Sparse Core Ops, SparseCore 0:
  226.0 60.9 reduce-scatter.1
